TPU v7x, 512 devices: a whole 4x4x16 slice. The times are simulated.
512 devices in a mesh: dp: 32 (over z_hi, x, core), tensor: 16 (over z_lo, y).
Axes of the slice: x: 4, y: 4, z: 16 (z_hi: 4, z_lo: 4; z = z_hi * 4 + z_lo), core: 2. Of those that a mesh axis runs over, the one named last changes fastest.
Arguments:
- gate_pre: bfloat16 [16384, 12800], P('dp', 'tensor'), may hold values from -8 to 8
- up_pre: bfloat16 [16384, 12800], P('dp', 'tensor'), may hold values from -6 to 6
- cotangent: bfloat16 [16384, 2560], P(('dp', 'tensor')), may hold values from -24 to 24
- down_weight: bfloat16 [12800, 2560], P('tensor', 'dp'), may hold values from -0.0546875 to 0.0546875
Outputs:
- grad_gate: bfloat16 [16384, 12800], P('dp', 'tensor')
- grad_up: bfloat16 [16384, 12800], P('dp', 'tensor')
- grad_down: bfloat16 [12800, 2560], P('tensor', 'dp')
- left_stat: float32 [16, 4, 800, 800], P('tensor', None, 'dp')
- right_stat: float32 [16, 4, 640, 640], P('tensor', None, 'dp')
All inputs are finite; a program needn't handle non-finite values.
Results may differ from a plain program's by a relative error of at most 0.025.
Values may be sent and summed in bfloat16 or wider, within the bound.
A program may use at most 64 MiB of HBM per device.

v0:
```python
import math

import jax
import jax.numpy as jnp
from jax import lax
from jax.sharding import PartitionSpec as P

D = 2560
BR = 800
CB = 640


def body(gate_pre, up_pre, cotangent, down_weight):
    tok_rows = gate_pre.shape[0]
    ff_local = gate_pre.shape[1]
    dp_count = lax.axis_size("dp")
    dp_index = lax.axis_index("dp")
    scale = 1.0 / math.sqrt(tok_rows * dp_count)
    full_cot = lax.all_gather(cotangent, "tensor", axis=0, tiled=True)
    gate_f = gate_pre.astype(jnp.float32)
    up_f = up_pre.astype(jnp.float32)
    sig = jax.nn.sigmoid(gate_f)
    act = gate_f * sig
    hidden = (act * up_f).astype(jnp.bfloat16)
    cols = full_cot
    dh = lax.dot_general(
        cols,
        lax.all_gather(down_weight, "dp", axis=1, tiled=True),
        (((1,), (1,)), ((), ())),
        preferred_element_type=jnp.float32,
    )
    grad_up = (dh * act).astype(jnp.bfloat16)
    grad_gate = (dh * up_f * sig * (1.0 + gate_f * (1.0 - sig))).astype(jnp.bfloat16)
    cols = full_cot
    owned = lax.psum_scatter(
        (
            lax.dot_general(
                cols, hidden, (((0,), (0,)), ((), ())), preferred_element_type=jnp.float32
            )
            * scale
        ).astype(jnp.bfloat16),
        "dp",
        scatter_dimension=0,
        tiled=True,
    )
    whole = lax.all_gather(owned, "dp", axis=0, tiled=True)
    grad_down = owned.T
    col_blocks = D // CB
    row_blocks = ff_local // BR
    blocks = whole.reshape(col_blocks, CB, row_blocks, BR)
    left_rows = BR // dp_count
    mine_left = lax.dynamic_slice_in_dim(blocks, dp_index * left_rows, left_rows, 3)
    left_stat = (
        jnp.einsum("ckri,ckrj->rcij", mine_left, blocks, preferred_element_type=jnp.float32) / CB
    )
    right_rows = CB // dp_count
    mine_right = lax.dynamic_slice_in_dim(blocks, dp_index * right_rows, right_rows, 1)
    right_stat = (
        jnp.einsum("cari,cbri->rcab", mine_right, blocks, preferred_element_type=jnp.float32) / BR
    )
    return (grad_gate, grad_up, grad_down, left_stat, right_stat)


def solution(mesh):
    return jax.shard_map(
        body,
        mesh=mesh,
        in_specs=(
            P("dp", "tensor"),
            P("dp", "tensor"),
            P(("dp", "tensor"), None),
            P("tensor", "dp"),
        ),
        out_specs=(
            P("dp", "tensor"),
            P("dp", "tensor"),
            P("tensor", "dp"),
            P("tensor", None, "dp", None),
            P("tensor", None, "dp", None),
        ),
        check_vma=False,
    )
```

profile of v0, /device:TPU:1, one launch (start us, length us, event | category | flops | bytes accessed | tf_op | source)
XLA Modules:
  0.0 476.0 jit_solution(3967858845956220404)
XLA Ops:
  7.2 0.0 all-gather.4.cloned.1.call-start
  7.2 0.7 all-gather.4.cloned.1.call-update
  7.9 0.0 reduce-scatter.4.cloned.1.call-start
  7.9 87.7 %all-gather.4.cloned.1.call-done = bf16[512,2560]{1,0:T(8,128)(2,1)} async-done(((bf16[32,2560]{1,0:T(8,128)(2,1)}), bf16[512,2560]{1,0:T(8,128)(2,1)}) %all-gather.4.cloned.1.call-update) | async-done | bytes 2621456 | tf_op jit(solution)/shard_map/all_gather | solution.py:19
  95.6 6.6 %fusion = bf16[2560,800]{0,1:T(8,128)(2,1)} fusion(bf16[512,2560]{1,0:T(8,128)(2,1)} %all-gather.4.cloned.1.call-done, bf16[512,800]{0,1:T(8,128)(2,1)} %param.5, bf16[512,800]{0,1:T(8,128)(2,1)} %param.4), kind=kOutput, calls=%fused_computation.1 | convolution fusion | flops 2104524800 | bytes 8355840 | tf_op jit(solution)/shard_map/dot_general | solution.py:37
  102.2 7.3 %copy.32 = bf16[2560,800]{1,0:T(8,128)(2,1)} copy(bf16[2560,800]{0,1:T(8,128)(2,1)} %fusion) | data formatting | bytes 8192000
  109.5 0.0 copy-start.1
  109.5 0.0 copy-start.2
  109.5 0.0 reduce-scatter.4.cloned.1.call-update
  109.5 0.0 all-gather.6.cloned.1.call-start
  109.6 0.7 all-gather.6.cloned.1.call-update
  110.3 0.0 all-gather.8.cloned.1.call-start
  110.3 154.1 %reduce-scatter.4.cloned.1.call-done = bf16[80,800]{1,0:T(8,128)(2,1)} async-done(((bf16[2560,800]{1,0:T(8,128)(2,1)}), bf16[80,800]{1,0:T(8,128)(2,1)}) %reduce-scatter.4.cloned.1.call-update) | async-done | bytes 128016 | tf_op jit(solution)/shard_map/reduce_scatter | solution.py:35
  264.4 0.0 all-gather.8.cloned.1.call-update
  264.4 100.2 %all-gather.6.cloned.1.call-done = bf16[800,2560]{0,1:T(8,128)(2,1)} async-done(((bf16[800,80]{0,1:T(8,128)(2,1)}), bf16[800,2560]{0,1:T(8,128)(2,1)}) %all-gather.6.cloned.1.call-update) | async-done | bytes 4096016 | tf_op jit(solution)/shard_map/all_gather | solution.py:28
  364.6 0.0 copy-done.1
  364.6 0.0 copy-done.2
  364.6 6.6 %multiply_convert_fusion.1 = (bf16[512,800]{0,1:T(8,128)(2,1)}, bf16[512,800]{0,1:T(8,128)(2,1)}) fusion(bf16[512,800]{0,1:T(8,128)(2,1)S(1)} %copy-done.2, bf16[512,800]{0,1:T(8,128)(2,1)} %param.5, bf16[512,2560]{1,0:T(8,128)(2,1)S(1)} %copy-done.1, bf16[800,2560]{0,1:T(8,128)(2,1)} %all-gather.6.cloned.1.call-done), kind=kOutput, calls=%fused_computation.15 | convolution fusion | flops 2103296000 | bytes 9994240 | tf_op jit(solution)/shard_map/dot_general | solution.py:26
  371.3 91.1 %all-gather.8.cloned.1.call-done = bf16[2560,800]{1,0:T(8,128)(2,1)} async-done(((bf16[80,800]{1,0:T(8,128)(2,1)}), bf16[2560,800]{1,0:T(8,128)(2,1)}) %all-gather.8.cloned.1.call-update) | async-done | bytes 4096016 | tf_op jit(solution)/shard_map/all_gather | solution.py:46
  462.4 4.1 fusion.9
  466.4 1.0 copy.27
  467.4 0.0 copy-done
  467.4 1.3 fusion.10
  468.7 0.7 copy.28
  (1 shorter events, 0.0 us)
Async XLA Ops:
  7.2 88.5 %all-gather.4.cloned.1.call-start = ((), (), s32[]{:S(2)}) async-start(), calls=%async_computation.1 | async-start | bytes 2785280 | tf_op jit(solution)/shard_map/all_gather | solution.py:19
  7.9 256.5 %reduce-scatter.4.cloned.1.call-start = ((), (), s32[]{:S(2)}) async-start(), calls=%async_computation.4 | async-start | bytes 4730880 | tf_op jit(solution)/shard_map/reduce_scatter | solution.py:35
  109.5 255.1 %copy-start.1 = (bf16[512,2560]{1,0:T(8,128)(2,1)S(1)}, bf16[512,2560]{1,0:T(8,128)(2,1)}, u32[]{:S(2)}) copy-start(bf16[512,2560]{1,0:T(8,128)(2,1)} %all-gather.4.cloned.1.call-done) | copy-start | bytes 7864324
  109.5 255.1 %copy-start.2 = (bf16[512,800]{0,1:T(8,128)(2,1)S(1)}, bf16[512,800]{0,1:T(8,128)(2,1)}, u32[]{:S(2)}) copy-start(bf16[512,800]{0,1:T(8,128)(2,1)} %param.4) | copy-start | bytes 2457604
  109.5 255.1 %all-gather.6.cloned.1.call-start = ((), (), s32[]{:S(2)}) async-start(), calls=%async_computation.2 | async-start | bytes 4730880 | tf_op jit(solution)/shard_map/all_gather | solution.py:28
  110.3 352.1 %all-gather.8.cloned.1.call-start = ((), (), s32[]{:S(2)}) async-start(), calls=%async_computation.3 | async-start | bytes 4730880 | tf_op jit(solution)/shard_map/all_gather | solution.py:46
  462.4 5.1 %copy-start = (bf16[2560,800]{1,0:T(8,128)(2,1)S(1)}, bf16[2560,800]{1,0:T(8,128)(2,1)}, u32[]{:S(2)}) copy-start(bf16[2560,800]{1,0:T(8,128)(2,1)} %all-gather.8.cloned.1.call-done) | copy-start | bytes 12288004
Sparse Core Ops, SparseCore 0:
  10.1 85.5 all-gather.3
  109.6 154.6 reduce-scatter.3
  267.6 97.0 all-gather.5
  368.2 94.0 all-gather.7
where the time goes:
time: 476 us
  waiting for transfers between devices  434 us (91%)
  matrix products  18.6 us (4%)
  between operations  13.8 us (3%)
  local copies, waits for them, and re-layouts  9 us (2%)
    reduce_scatter x1, waiting for transfers between devices, body(): lax.psum_scatter((lax.dot_general(cols, hidden, (((0,), (0,)), ((), ())),...  154 us
    all_gather x1, waiting for transfers between devices, body(): lax.all_gather(down_weight, 'dp', axis=1, tiled=True)  100 us
    all_gather x1, waiting for transfers between devices, body(): whole = lax.all_gather(owned, 'dp', axis=0, tiled=True)  91.1 us
    all_gather x1, waiting for transfers between devices, body(): full_cot = lax.all_gather(cotangent, 'tensor', axis=0, tiled=True)  87.7 us
  transfers between devices with their start and end apart: 4, of which 4 were waited for; matrix products, arithmetic and copies ran while one was open for 1% of the time, Pallas kernels for 0%

commit v1 on v0

v1 whole, which is shorter than its diff:
```python
import jax
import jax.numpy as jnp
from jax import lax
from jax.experimental import pallas as pl
from jax.experimental.pallas import tpu as pltpu
from jax.sharding import PartitionSpec as P

D = 2560
BR = 800
CB = 640
TOK = 512
SCALE = 1.0 / 128.0
MESH = pl.DeviceIdType.MESH
F32 = jnp.float32
BF16 = jnp.bfloat16
NSEM = 120
ORDER = (2, 1, 3, 0)


def kernel(gate_h, up_h, cot_h, w_h, gg_h, gu_h, gd_ref, left_ref, right_ref,
           gate, up, wv, cot, ht, act, fac, wt, tb, cr, cs, xr, zs, z1r, z2r,
           gs, g2, sl, rl, sr, rr, acc, gg, gu, ssem, rsem, lsem):
    dp = lax.axis_index("dp")
    te = lax.axis_index("tensor")
    zh = dp // 8
    x = (dp // 2) % 4
    k = dp % 2
    zl = te // 4
    y = te % 4

    def at_zh(e):
        return (((zh + e) % 4) * 8 + x * 2 + k, te)

    def at_x(d):
        return (zh * 8 + ((x + d) % 4) * 2 + k, te)

    def at_core():
        return (zh * 8 + x * 2 + (1 - k), te)

    def at_zl(d):
        return (dp, (zl + d) * 4 + y)

    def at_y(d):
        return (dp, zl * 4 + (y + d) % 4)

    count = [0]
    sent = []

    def rcopy(src, dst, dev, sem=None):
        if sem is None:
            sem = count[0]
            count[0] += 1
        return pltpu.make_async_remote_copy(
            src_ref=src, dst_ref=dst, send_sem=ssem.at[sem], recv_sem=rsem.at[sem],
            device_id=dev, device_id_type=MESH)

    def send(src, dst, dev):
        c = rcopy(src, dst, dev)
        c.start()
        sent.append(c)
        return c

    loads_c = []
    for n, o in enumerate(ORDER):
        col = pl.multiple_of(((zh + o) % 4) * CB, CB)
        c = pltpu.make_async_copy(cot_h.at[:, pl.ds(col, CB)], cot.at[o, 0, y], lsem.at[n])
        c.start()
        loads_c.append(c)
    load_w = pltpu.make_async_copy(w_h, wv, lsem.at[4])
    load_w.start()
    loads_g = []
    for r in range(4):
        row = pl.multiple_of(((zl + r) % 4) * 128, 128)
        a = pltpu.make_async_copy(gate_h.at[pl.ds(row, 128)], gate.at[pl.ds(r * 128, 128)], lsem.at[5 + r])
        b = pltpu.make_async_copy(up_h.at[pl.ds(row, 128)], up.at[pl.ds(r * 128, 128)], lsem.at[9 + r])
        a.start()
        b.start()
        loads_g.append((a, b))

    bar = pltpu.get_barrier_semaphore()

    def greet(dev):
        pl.semaphore_signal(bar, inc=1, device_id=dev, device_id_type=MESH)

    greet(at_core())
    for d in (1, 2, 3):
        greet(at_y(d))
        greet(at_x(d))
        greet(at_zh(d))

    @pl.when(zl > 0)
    def _():
        greet(at_zl(-1))

    @pl.when(zl < 3)
    def _():
        greet(at_zl(1))

    load_w.wait()
    eye = (lax.broadcasted_iota(jnp.int32, (80, 80), 0) == lax.broadcasted_iota(jnp.int32, (80, 80), 1))
    wt[0, x, k] = lax.dot_general(
        eye.astype(F32).astype(BF16), wv[...], (((1,), (1,)), ((), ())),
        preferred_element_type=F32).astype(BF16)
    for c in loads_c:
        c.wait()

    pl.semaphore_wait(bar, 10 + jnp.where(zl > 0, 1, 0) + jnp.where(zl < 3, 1, 0))

    line_sem = {}
    for o in ORDER:
        for j in (1, 2, 3):
            for d in (1, -1):
                line_sem[o, j, d] = count[0]
                count[0] += 1

    def line_copy(o, j, d):
        if d == 1:
            s, t = (4 - (j - 1)) % 4, 4 - j
        else:
            s, t = j - 1, j
        return rcopy(cot.at[o, s, y], cot.at[o, t, y], at_zl(d), line_sem[o, j, d])

    def line_sends(o, j, d):
        if d == 1:
            return jnp.logical_and(zl - (j - 1) >= 0, zl < 3)
        return jnp.logical_and(zl + (j - 1) <= 3, zl > 0)

    def line_send(o, j):
        for d in (1, -1):
            @pl.when(line_sends(o, j, d))
            def _(d=d):
                line_copy(o, j, d).start()

    def line_recv(o, j):
        @pl.when(zl - j >= 0)
        def _():
            line_copy(o, j, 1).wait_recv()

        @pl.when(zl + j <= 3)
        def _():
            line_copy(o, j, -1).wait_recv()

    y_own = {}
    y_rest = {}
    for o in ORDER:
        line_send(o, 1)
        y_own[o] = [send(cot.at[o, 0, y], cot.at[o, 0, y], at_y(d)) for d in (1, 3, 2)]

    w_x = {}
    w_core = {}

    def w_to_x(o):
        w_x[o] = [send(wt.at[o, x, k], wt.at[o, x, k], at_x(d)) for d in (1, 3, 2)]

    def w_to_core(o):
        for c in w_x[o]:
            c.wait_recv()
        w_core[o] = send(wt.at[o, :, k], wt.at[o, :, k], at_core())

    w_to_x(0)

    def hidden(r):
        rows = pl.ds(r * 128, 128)
        loads_g[r][0].wait()
        loads_g[r][1].wait()
        g = gate[rows, :].astype(F32)
        u = up[rows, :].astype(F32)
        sig = jax.nn.sigmoid(g)
        a = g * sig
        act[rows, :] = a
        fac[rows, :] = u * sig * (1.0 + g * (1.0 - sig))
        ht[:, rows] = (a * u).astype(BF16).T

    def line_step(o, j):
        line_recv(o, j)
        if j < 3:
            line_send(o, j + 1)
        else:
            y_rest[o] = [send(cot.at[o, pl.ds(1, 3), y], cot.at[o, pl.ds(1, 3), y], at_y(d)) for d in (1, 3, 2)]

    hidden(0)
    line_step(2, 1)
    line_step(1, 1)
    hidden(1)
    line_step(2, 2)
    line_step(3, 1)
    line_step(1, 2)
    hidden(2)
    line_step(2, 3)
    line_step(0, 1)
    line_step(3, 2)
    line_step(1, 3)
    hidden(3)
    line_step(0, 2)
    line_step(3, 3)
    line_step(0, 3)

    w_up = send(wt.at[0, x, k], wt.at[3, x, k], at_zh(1))
    w_dn = send(wt.at[0, x, k], wt.at[1, x, k], at_zh(3))

    tb[:, pl.ds(4000, 96), :] = jnp.zeros((4, 96, 128), BF16)
    core_c = {}
    x_c = {}

    def stage1(o):
        for c in y_own[o]:
            c.wait_recv()
        for c in y_rest[o]:
            c.wait_recv()

        @pl.loop(0, 5)
        def _(i):
            m = pl.multiple_of(i * 160, 160)
            t = jnp.dot(ht[pl.ds(m, 160), :], cot[o].reshape(TOK, CB), preferred_element_type=F32) * SCALE
            for j in range(5):
                row = pl.multiple_of(j * 800 + i * 160, 160)
                tb[o, pl.ds(row, 160), :] = t[:, j * 128:(j + 1) * 128].astype(BF16)

        other = pl.multiple_of((1 - k) * 2048, 2048)
        core_c[o] = send(tb.at[o, pl.ds(other, 2048)], cr.at[o], at_core())

    def stage2(o):
        core_c[o].wait_recv()
        mine = pl.multiple_of(k * 2048, 2048)

        @pl.loop(0, 4)
        def _(i):
            m = pl.multiple_of(i * 512, 512)
            s = tb[o, pl.ds(mine + m, 512), :].astype(F32) + cr[o, pl.ds(m, 512), :].astype(F32)
            cs[o, i] = s.astype(BF16)

        x_c[o] = [send(cs.at[o, (x + d) % 4], xr.at[o, d - 1], at_x(d)) for d in (1, 3, 2)]

    def x_sum(o):
        for c in x_c[o]:
            c.wait_recv()
        return (cs[o, x].astype(F32) + xr[o, 0].astype(F32)) + (xr[o, 1].astype(F32) + xr[o, 2].astype(F32))

    z_c = {}

    def stage3(o):
        p = x_sum(o)
        if o == 2:
            zs[0] = p.astype(BF16)
            z_c["up"] = send(zs.at[0, pl.ds(0, 256)], z1r.at[0], at_zh(1))
            z_c["dn"] = send(zs.at[0, pl.ds(256, 256)], z1r.at[1], at_zh(3))
        elif o == 1:
            z_c["up"].wait_recv()
            zs[1, pl.ds(0, 256)] = (p[:256] + z1r[0].astype(F32)).astype(BF16)
            zs[1, pl.ds(256, 256)] = p[256:].astype(BF16)
            z_c["up2"] = send(zs.at[1], z2r.at[0], at_zh(1))
        elif o == 3:
            z_c["dn"].wait_recv()
            zs[2, pl.ds(0, 256)] = p[:256].astype(BF16)
            zs[2, pl.ds(256, 256)] = (p[256:] + z1r[1].astype(F32)).astype(BF16)
            z_c["dn2"] = send(zs.at[2], z2r.at[1], at_zh(3))
        else:
            z_c["up2"].wait_recv()
            z_c["dn2"].wait_recv()
            own = pl.multiple_of((k * 4 + x) * 512, 512)
            gs[pl.ds(own, 512), :] = (p + (z2r[0].astype(F32) + z2r[1].astype(F32))).astype(BF16)

    stage1(2)
    stage2(2)
    stage1(1)
    stage2(1)
    stage3(2)
    w_to_core(0)
    stage1(3)
    stage2(3)
    stage3(1)
    stage1(0)
    stage2(0)
    stage3(3)

    w_up.wait_recv()
    w_up2 = send(wt.at[3, x, k, pl.ds(0, 48)], wt.at[2, x, k, pl.ds(0, 48)], at_zh(1))
    w_dn.wait_recv()
    w_dn2 = send(wt.at[1, x, k, pl.ds(48, 32)], wt.at[2, x, k, pl.ds(48, 32)], at_zh(3))
    w_to_x(1)

    def dh_step(o, first):
        @pl.loop(0, 2)
        def _(i):
            c = cot[o, pl.ds(i * 2, 2)].reshape(256, CB)
            t = jnp.dot(c, wt[o].reshape(CB, BR), preferred_element_type=F32)
            rows = pl.ds(pl.multiple_of(i * 256, 256), 256)
            if first:
                acc[rows, :] = t
            else:
                acc[rows, :] += t

    w_core[0].wait_recv()
    dh_step(0, True)

    stage3(0)
    own = pl.multiple_of((k * 4 + x) * 512, 512)
    g_x = [send(gs.at[pl.ds(own, 512)], gs.at[pl.ds(own, 512)], at_x(d)) for d in (1, 3, 2)]
    w_to_x(3)
    w_to_core(1)
    for c in g_x:
        c.wait_recv()
    half = pl.multiple_of(k * 2048, 2048)
    g_core = send(gs.at[pl.ds(half, 2048)], gs.at[pl.ds(half, 2048)], at_core())
    w_up2.wait_recv()
    w_dn2.wait_recv()
    w_to_x(2)
    g_core.wait_recv()
    for j in range(5):
        g2[:, j * 128:(j + 1) * 128] = gs[pl.ds(j * 800, 800), :]

    def pick(n, per_zh, per_x, per_k, used):
        s = lax.broadcasted_iota(jnp.int32, (128, n), 0)
        r = lax.broadcasted_iota(jnp.int32, (128, n), 1)
        i = s & 31
        want = ((zh + (s >> 5)) & 3) * per_zh + x * per_x + k * per_k + i
        return jnp.logical_and(r == want, i < used).astype(F32).astype(BF16)

    gm = g2[...]
    rows_l = jnp.dot(pick(BR, 200, 50, 25, 25), gm, preferred_element_type=F32).astype(BF16)
    lt = lax.dot_general(rows_l, gm, (((1,), (1,)), ((), ())), preferred_element_type=F32) / CB
    cols_r = lax.dot_general(
        pick(CB, 160, 40, 20, 20), gm, (((1,), (1,)), ((), ())), preferred_element_type=F32).astype(BF16)
    rt = jnp.dot(cols_r, gm, preferred_element_type=F32) / BR
    for e in (1, 2, 3):
        sl[e - 1] = lt[32 * e:32 * e + 32].astype(BF16)
        sr[e - 1] = rt[32 * e:32 * e + 32].astype(BF16)
    st = {}
    for e in (2, 1, 3):
        st[e] = (send(sl.at[e - 1], rl.at[e - 1], at_zh(e)), send(sr.at[e - 1], rr.at[e - 1], at_zh(e)))
    left_ref[zh] = lt[:25]
    right_ref[zh] = rt[:20]
    sel = (lax.broadcasted_iota(jnp.int32, (CB, 80), 0)
           == lax.broadcasted_iota(jnp.int32, (CB, 80), 1) + (2 * x + k) * 80)
    gd_ref[...] = jnp.dot(gm, sel.astype(F32).astype(BF16), preferred_element_type=F32).astype(BF16)

    w_core[1].wait_recv()
    dh_step(1, False)
    w_to_core(3)
    w_core[3].wait_recv()
    dh_step(3, False)
    w_to_core(2)
    w_core[2].wait_recv()
    stores = []
    for i in range(2):
        c = cot[2, pl.ds(i * 2, 2)].reshape(256, CB)
        rows = pl.ds(i * 256, 256)
        dh = acc[rows, :] + jnp.dot(c, wt[2].reshape(CB, BR), preferred_element_type=F32)
        gu[rows, :] = (dh * act[rows, :]).astype(BF16)
        gg[rows, :] = (dh * fac[rows, :]).astype(BF16)
        for r in (2 * i, 2 * i + 1):
            row = pl.multiple_of(((zl + r) % 4) * 128, 128)
            a = pltpu.make_async_copy(gg.at[pl.ds(r * 128, 128)], gg_h.at[pl.ds(row, 128)], lsem.at[13 + r])
            b = pltpu.make_async_copy(gu.at[pl.ds(r * 128, 128)], gu_h.at[pl.ds(row, 128)], lsem.at[17 + r])
            a.start()
            b.start()
            stores += [a, b]

    for e in (1, 3, 2):
        st[e][0].wait_recv()
        st[e][1].wait_recv()
        c = (zh + 4 - e) % 4
        left_ref[c] = rl[e - 1, pl.ds(0, 32), :].astype(F32)[:25]
        right_ref[c] = rr[e - 1, pl.ds(0, 32), :].astype(F32)[:20]

    for c in stores:
        c.wait()
    for c in sent:
        c.wait_send()
    for o in ORDER:
        for j in (1, 2, 3):
            for d in (1, -1):
                @pl.when(line_sends(o, j, d))
                def _(o=o, j=j, d=d):
                    line_copy(o, j, d).wait_send()
    assert count[0] <= NSEM


def body(gate_pre, up_pre, cotangent, down_weight):
    anyspec = pl.BlockSpec(memory_space=pl.ANY)
    vspec = pl.BlockSpec(memory_space=pltpu.VMEM)
    v = pltpu.VMEM
    out = pl.pallas_call(
        kernel,
        out_shape=(
            jax.ShapeDtypeStruct((TOK, BR), BF16),
            jax.ShapeDtypeStruct((TOK, BR), BF16),
            jax.ShapeDtypeStruct((BR, 80), BF16),
            jax.ShapeDtypeStruct((4, 25, BR), F32),
            jax.ShapeDtypeStruct((4, 20, CB), F32),
        ),
        in_specs=[anyspec] * 4,
        out_specs=(anyspec, anyspec, vspec, vspec, vspec),
        scratch_shapes=[
            v((TOK, BR), BF16),
            v((TOK, BR), BF16),
            v((BR, 80), BF16),
            v((4, 4, 4, 32, CB), BF16),
            v((BR, TOK), BF16),
            v((TOK, BR), F32),
            v((TOK, BR), F32),
            v((4, 4, 2, 80, BR), BF16),
            v((4, 4096, 128), BF16),
            v((4, 2048, 128), BF16),
            v((4, 4, 512, 128), BF16),
            v((4, 3, 512, 128), BF16),
            v((3, 512, 128), BF16),
            v((2, 256, 128), BF16),
            v((2, 512, 128), BF16),
            v((4096, 128), BF16),
            v((BR, CB), BF16),
            v((3, 32, BR), BF16),
            v((3, 32, BR), BF16),
            v((3, 32, CB), BF16),
            v((3, 32, CB), BF16),
            v((TOK, BR), F32),
            v((TOK, BR), BF16),
            v((TOK, BR), BF16),
            pltpu.SemaphoreType.DMA((NSEM,)),
            pltpu.SemaphoreType.DMA((NSEM,)),
            pltpu.SemaphoreType.DMA((21,)),
        ],
        compiler_params=pltpu.CompilerParams(
            collective_id=0, has_side_effects=True, vmem_limit_bytes=56 * 2**20),
        cost_estimate=pl.CostEstimate(flops=4_600_000_000, bytes_accessed=6_000_000, transcendentals=410_000),
    )(gate_pre, up_pre, cotangent, down_weight)
    return out[0], out[1], out[2], out[3][None], out[4][None]


def solution(mesh):
    return jax.shard_map(
        body,
        mesh=mesh,
        in_specs=(
            P("dp", "tensor"),
            P("dp", "tensor"),
            P(("dp", "tensor"), None),
            P("tensor", "dp"),
        ),
        out_specs=(
            P("dp", "tensor"),
            P("dp", "tensor"),
            P("tensor", "dp"),
            P("tensor", None, "dp", None),
            P("tensor", None, "dp", None),
        ),
        check_vma=False,
    )
```

time: 476 us -> 115 us (0.24)
  waiting for transfers between devices: 434 us -> 0 us
  Pallas kernels: 0 us -> 103 us
  matrix products: 18.6 us -> 0 us
  between operations: 13.8 us -> 0.67 us
    all_gather x3 -> x0, waiting for transfers between devices: 279 us -> none  [the longest x1 100 us: body(): lax.all_gather(down_weight, 'dp', axis=1, tiled=True)]
    reduce_scatter x1 -> x0, waiting for transfers between devices: 154 us -> none  [body(): lax.psum_scatter((lax.dot_general(cols, hidden, (((0,), (0,)), ((), ())),...]
    pallas_call x0 -> x1, Pallas kernels: none -> 103 us  [body(): pl.pallas_call(kernel, out_shape=(jax.ShapeDtypeStruct((TOK, BR), BF16),...]
    dot_general x4 -> x0, matrix products: 18.6 us -> none  [the longest x1 6.64 us: body(): lax.dot_general(cols, lax.all_gather(down_weight, 'dp', axis=1, tiled=Tru...]
    unnamed x9 -> x18, local copies, waits for them, and re-layouts: 9 us -> 11.2 us
  transfers between devices with their start and end apart: 4 -> 0, of which waited for: 4 -> 0; matrix products, arithmetic and copies ran while one was open for 1% -> 0% of each run, Pallas kernels for 0% -> 0%
where the time goes in v1:
time: 115 us; the launch traced here: 114 us
  Pallas kernels  103 us (90%)
  local copies, waits for them, and re-layouts  11.2 us (10%)
    pallas_call x1, Pallas kernels, body(): pl.pallas_call(kernel, out_shape=(jax.ShapeDtypeStruct((TOK, BR), BF16),...  103 us
    unnamed x18, local copies, waits for them, and re-layouts  11.2 us

profile of v1, /device:TPU:1, one launch (start us, length us, event | category | flops | bytes accessed | tf_op | source)
XLA Modules:
  0.0 114.4 jit_solution(1251100969374206774)
XLA Ops:
  0.6 1.7 %copy.11.w_h = bf16[800,80]{1,0:T(8,128)(2,1)} copy(bf16[800,80]{0,1:T(8,128)(2,1)} %param.7) | data formatting | bytes 256000 | tf_op args[3]
  2.4 0.0 copy-start.1
  2.4 2.3 %copy.9.gate_h = bf16[512,800]{1,0:T(8,128)(2,1)} copy(bf16[512,800]{0,1:T(8,128)(2,1)} %param.4) | data formatting | bytes 1638400 | tf_op args[0]
  4.6 0.0 copy-done.1
  4.6 1.3 %copy.10.up_h = bf16[512,800]{1,0:T(8,128)(2,1)} copy(bf16[512,800]{0,1:T(8,128)(2,1)S(1)} %copy-done.1) | data formatting | bytes 1638400 | tf_op args[1]
  5.9 102.5 %shard_map.83 = (bf16[512,800]{1,0:T(8,128)(2,1)}, bf16[512,800]{1,0:T(8,128)(2,1)}, bf16[800,80]{1,0:T(8,128)(2,1)}, f32[4,25,800]{2,1,0:T(8,128)}, f32[4,20,640]{2,1,0:T(8,128)}) custom-call(bf16[512,800]{1,0:T(8,128)(2,1)} %copy.9.gate_h, bf16[512,800]{1,0:T(8,128)(2,1)} %copy.10.up_h, bf16[32,2560]{1,0:T(8,128)(2,1)} %cot_h.1, bf16[800,80]{1,0:T(8,128)(2,1)} %copy.11.w_h), custom_call_target="tpu_custom_call" | custom-call | flops 4600000000 | bytes 6000000 | tf_op jit(solution)/shard_map/pallas_call | solution.py:383
  108.4 0.0 copy-start.4
  108.5 0.0 copy-start.3
  108.5 0.0 copy-start.2
  108.5 2.2 %copy.12 = bf16[512,800]{0,1:T(8,128)(2,1)} copy(bf16[512,800]{1,0:T(8,128)(2,1)} %get-tuple-element.15) | data formatting | bytes 1638400
  110.7 0.0 copy-done.4
  110.7 0.0 copy-start
  110.7 0.8 copy.14
  111.5 0.0 copy-done.3
  111.5 0.7 copy.16
  112.2 0.0 copy-done.2
  112.2 1.0 copy.15
  113.2 0.0 copy-done
  113.2 1.2 %copy.13 = bf16[512,800]{0,1:T(8,128)(2,1)} copy(bf16[512,800]{1,0:T(8,128)(2,1)S(1)} %copy-done) | data formatting | bytes 1638400
Async XLA Ops:
  2.4 2.3 %copy-start.1 = (bf16[512,800]{0,1:T(8,128)(2,1)S(1)}, bf16[512,800]{0,1:T(8,128)(2,1)}, u32[]{:S(2)}) copy-start(bf16[512,800]{0,1:T(8,128)(2,1)} %param.5) | copy-start | bytes 2457604
  108.4 2.3 %copy-start.4 = (bf16[800,80]{1,0:T(8,128)(2,1)S(1)}, bf16[800,80]{1,0:T(8,128)(2,1)}, u32[]{:S(2)}) copy-start(bf16[800,80]{1,0:T(8,128)(2,1)} %get-tuple-element.17) | copy-start | bytes 384004
  108.5 3.0 %copy-start.3 = (f32[4,20,640]{2,1,0:T(8,128)S(1)}, f32[4,20,640]{2,1,0:T(8,128)}, u32[]{:S(2)}) copy-start(f32[4,20,640]{2,1,0:T(8,128)} %get-tuple-element.14) | copy-start | bytes 614404
  108.5 3.8 %copy-start.2 = (f32[4,25,800]{2,1,0:T(8,128)S(1)}, f32[4,25,800]{2,1,0:T(8,128)}, u32[]{:S(2)}) copy-start(f32[4,25,800]{2,1,0:T(8,128)} %get-tuple-element.13) | copy-start | bytes 960004
  110.7 2.5 %copy-start = (bf16[512,800]{1,0:T(8,128)(2,1)S(1)}, bf16[512,800]{1,0:T(8,128)(2,1)}, u32[]{:S(2)}) copy-start(bf16[512,800]{1,0:T(8,128)(2,1)} %get-tuple-element.16) | copy-start | bytes 2457604

commit v2 on v1

v2 whole, which is shorter than its diff:
```python
import jax
import jax.numpy as jnp
from jax import lax
from jax.experimental import pallas as pl
from jax.experimental.pallas import tpu as pltpu
from jax.sharding import PartitionSpec as P

D = 2560
BR = 800
CB = 640
TOK = 512
SCALE = 1.0 / 128.0
MESH = pl.DeviceIdType.MESH
F32 = jnp.float32
BF16 = jnp.bfloat16
NSEM = 160
PARTS = ((0, 384, 3, 0, 304, 0, 0, 160), (384, 256, 2, 2432, 208, 1216, 304, 112))
SUBS = ((2, 0), (2, 1), (1, 0), (3, 0), (1, 1), (3, 1), (0, 0), (0, 1))
ORDER = (2, 1, 3, 0)


def kernel(gate_h, up_h, cot_h, w_h, gg_h, gu_h, gd_ref, left_ref, right_ref,
           gate, up, cot, ht, act, fac, wt, tb, cr, cs, xr, zs, z1r, z2r,
           gs, g2, sp, rp, lt4, rt4, acc, gg, gu, ssem, rsem, lsem):
    dp = lax.axis_index("dp")
    te = lax.axis_index("tensor")
    zh = dp // 8
    x = (dp // 2) % 4
    k = dp % 2
    zl = te // 4
    y = te % 4

    def at_zh(e):
        return (((zh + e) % 4) * 8 + x * 2 + k, te)

    def at_x(d):
        return (zh * 8 + ((x + d) % 4) * 2 + k, te)

    def at_core():
        return (zh * 8 + x * 2 + (1 - k), te)

    def at_zl(d):
        return (dp, (zl + d) * 4 + y)

    def at_y(d):
        return (dp, zl * 4 + (y + d) % 4)

    count = [0]
    sent = []

    def rcopy(src, dst, dev, sem=None):
        if sem is None:
            sem = count[0]
            count[0] += 1
        return pltpu.make_async_remote_copy(
            src_ref=src, dst_ref=dst, send_sem=ssem.at[sem], recv_sem=rsem.at[sem],
            device_id=dev, device_id_type=MESH)

    def send(src, dst, dev):
        c = rcopy(src, dst, dev)
        c.start()
        sent.append(c)
        return c

    loads_c = []
    for n, o in enumerate(ORDER):
        col = pl.multiple_of(((zh + o) % 4) * CB, CB)
        c = pltpu.make_async_copy(cot_h.at[:, pl.ds(col, CB)], cot.at[o, 0, y], lsem.at[n])
        c.start()
        loads_c.append(c)
    load_w = pltpu.make_async_copy(w_h, wt.at[0, x, k], lsem.at[4])
    load_w.start()
    loads_g = []
    for r in range(4):
        row = pl.multiple_of(((zl + r) % 4) * 128, 128)
        a = pltpu.make_async_copy(gate_h.at[:, pl.ds(row, 128)], gate.at[:, pl.ds(r * 128, 128)], lsem.at[5 + r])
        b = pltpu.make_async_copy(up_h.at[:, pl.ds(row, 128)], up.at[:, pl.ds(r * 128, 128)], lsem.at[9 + r])
        a.start()
        b.start()
        loads_g.append((a, b))

    bar = pltpu.get_barrier_semaphore()

    def greet(dev):
        pl.semaphore_signal(bar, inc=1, device_id=dev, device_id_type=MESH)

    greet(at_core())
    for d in (1, 2, 3):
        greet(at_y(d))
        greet(at_x(d))
        greet(at_zh(d))

    @pl.when(zl > 0)
    def _():
        greet(at_zl(-1))

    @pl.when(zl < 3)
    def _():
        greet(at_zl(1))

    load_w.wait()
    for c in loads_c:
        c.wait()

    pl.semaphore_wait(bar, 10 + jnp.where(zl > 0, 1, 0) + jnp.where(zl < 3, 1, 0))

    line_sem = {}
    for o in ORDER:
        for j in (1, 2, 3):
            for d in (1, -1):
                line_sem[o, j, d] = count[0]
                count[0] += 1

    def line_copy(o, j, d):
        if d == 1:
            s, t = (4 - (j - 1)) % 4, 4 - j
        else:
            s, t = j - 1, j
        return rcopy(cot.at[o, s, y], cot.at[o, t, y], at_zl(d), line_sem[o, j, d])

    def line_sends(o, j, d):
        if d == 1:
            return jnp.logical_and(zl - (j - 1) >= 0, zl < 3)
        return jnp.logical_and(zl + (j - 1) <= 3, zl > 0)

    def line_send(o, j):
        for d in (1, -1):
            @pl.when(line_sends(o, j, d))
            def _(d=d):
                line_copy(o, j, d).start()

    def line_recv(o, j):
        @pl.when(zl - j >= 0)
        def _():
            line_copy(o, j, 1).wait_recv()

        @pl.when(zl + j <= 3)
        def _():
            line_copy(o, j, -1).wait_recv()

    def y_pair(o, slots, y_from, half, cols):
        up = cot.at[o, slots, (y + y_from[0]) % 4, half[0], cols]
        dn = cot.at[o, slots, (y + y_from[1]) % 4, half[1], cols]
        return [send(up, up, at_y(1)), send(dn, dn, at_y(3))]

    whole = (pl.ds(0, 32), pl.ds(0, 32))
    halves = (pl.ds(0, 16), pl.ds(16, 16))
    y1 = {}
    y2 = {}

    def own_to_y():
        y1["own"] = y_pair(pl.ds(0, 4), pl.ds(0, 1), (0, 0), whole, pl.ds(0, CB))

    def own_relay():
        for c in y1["own"]:
            c.wait_recv()
        y2["own"] = y_pair(pl.ds(0, 4), pl.ds(0, 1), (3, 1), halves, pl.ds(0, CB))

    def rest_to_y(n):
        o, part = SUBS[n]
        y1[o, part] = y_pair(o, pl.ds(1, 3), (0, 0), whole, pl.ds(*PARTS[part][:2]))

    def rest_relay(n):
        o, part = SUBS[n]
        for c in y1[o, part]:
            c.wait_recv()
        y2[o, part] = y_pair(o, pl.ds(1, 3), (3, 1), halves, pl.ds(*PARTS[part][:2]))

    for o in ORDER[:3]:
        line_send(o, 1)
    own_to_y()

    w_x = {}
    w_core = {}

    def w_to_x(o):
        w_x[o] = [send(wt.at[o, x, k], wt.at[o, x, k], at_x(d)) for d in (1, 3, 2)]

    def w_to_core(o):
        for c in w_x[o]:
            c.wait_recv()
        w_core[o] = send(wt.at[o, :, k], wt.at[o, :, k], at_core())

    w_to_x(0)

    def hidden(r):
        cols = pl.ds(r * 128, 128)
        loads_g[r][0].wait()
        loads_g[r][1].wait()

        @pl.loop(0, 5)
        def _(i):
            rows = pl.ds(pl.multiple_of(i * 160, 160), 160)
            g = gate[rows, cols].astype(F32)
            u = up[rows, cols].astype(F32)
            sig = jax.nn.sigmoid(g)
            a = g * sig
            act[rows, cols] = a
            fac[rows, cols] = u * sig * (1.0 + g * (1.0 - sig))
            ht[rows, cols] = (a * u).astype(BF16)

    def line_step(o, j):
        line_recv(o, j)
        if j < 3:
            line_send(o, j + 1)

    hidden(0)
    line_step(2, 1)
    line_send(0, 1)
    line_step(1, 1)
    hidden(1)
    line_step(2, 2)
    line_step(3, 1)
    own_relay()
    hidden(2)
    line_step(0, 1)
    line_step(1, 2)
    line_step(2, 3)
    rest_to_y(0)
    rest_to_y(1)
    hidden(3)
    line_step(3, 2)
    line_step(0, 2)
    line_step(1, 3)
    rest_to_y(2)
    rest_relay(0)
    line_step(3, 3)
    rest_to_y(3)
    rest_relay(1)
    rest_to_y(4)
    line_step(0, 3)

    def w_z(name, src, dst, first, rows, e):
        w_zc[name] = send(wt.at[src, x, k, pl.ds(first, rows)], wt.at[dst, x, k, pl.ds(first, rows)], at_zh(e))

    w_zc = {}
    w_z("up", 0, 3, 0, 48, 1)
    w_z("dn", 0, 1, 48, 32, 3)
    w_z("up2", 0, 3, 48, 32, 1)
    w_z("dn2", 0, 1, 0, 48, 3)

    tb[:, pl.ds(2400, 32), :] = jnp.zeros((4, 32, 128), BF16)
    tb[:, pl.ds(4032, 64), :] = jnp.zeros((4, 64, 128), BF16)
    core_c = {}
    x_c = {}
    z_c = {}
    g_x = {}

    def at16(v):
        return pl.multiple_of(v, 16)

    def stage1(n):
        o, part = SUBS[n]
        c0, cols, tiles, base, rows, b2, b5, up_rows = PARTS[part]
        if n == 0:
            for c in y2["own"]:
                c.wait_recv()
        for c in y2[o, part]:
            c.wait_recv()

        @pl.loop(0, 2)
        def _(i):
            m = pl.multiple_of(i * 400, 16)
            c = cot[o, :, :, :, pl.ds(c0, cols)].reshape(TOK, cols)
            t = jnp.dot(ht[pl.ds(m, 400), :], c, preferred_element_type=F32) * SCALE
            for j in range(tiles):
                tb[o, pl.ds(at16(base + j * 800 + i * 400), 400), :] = t[:, j * 128:(j + 1) * 128].astype(BF16)

        core_c[n] = send(tb.at[o, pl.ds(at16(base + (1 - k) * (4 * rows)), 4 * rows)],
                         cr.at[o, pl.ds(b2, 4 * rows)], at_core())

    def stage2(n):
        o, part = SUBS[n]
        c0, cols, tiles, base, rows, b2, b5, up_rows = PARTS[part]
        core_c[n].wait_recv()

        @pl.loop(0, 4)
        def _(i):
            a = tb[o, pl.ds(at16(base + (k * 4 + i) * rows), rows), :]
            b = cr[o, pl.ds(at16(b2 + i * rows), rows), :]
            cs[o, pl.ds(at16(b2 + i * rows), rows), :] = (a.astype(F32) + b.astype(F32)).astype(BF16)

        x_c[n] = [send(cs.at[o, pl.ds(at16(b2 + ((x + d) % 4) * rows), rows)],
                       xr.at[o, d - 1, pl.ds(b5, rows)], at_x(d)) for d in (1, 3, 2)]

    def stage3(n):
        o, part = SUBS[n]
        c0, cols, tiles, base, rows, b2, b5, up_rows = PARTS[part]
        dn_rows = rows - up_rows
        for c in x_c[n]:
            c.wait_recv()
        here = pl.ds(b5, rows)
        up = pl.ds(b5, up_rows)
        dn = pl.ds(b5 + up_rows, dn_rows)
        p = cs[o, pl.ds(at16(b2 + x * rows), rows), :].astype(F32) + xr[o, 0, here].astype(F32)
        p = p + (xr[o, 1, here].astype(F32) + xr[o, 2, here].astype(F32))
        if o == 2:
            zs[0, here] = p.astype(BF16)
            z_c["up", part] = send(zs.at[0, up], z1r.at[0, up], at_zh(1))
            z_c["dn", part] = send(zs.at[0, dn], z1r.at[1, dn], at_zh(3))
        elif o == 1:
            z_c["up", part].wait_recv()
            zs[1, up] = (p[:up_rows] + z1r[0, up].astype(F32)).astype(BF16)
            zs[1, dn] = p[up_rows:].astype(BF16)
            z_c["up2", part] = send(zs.at[1, here], z2r.at[0, here], at_zh(1))
        elif o == 3:
            z_c["dn", part].wait_recv()
            zs[2, up] = p[:up_rows].astype(BF16)
            zs[2, dn] = (p[up_rows:] + z1r[1, dn].astype(F32)).astype(BF16)
            z_c["dn2", part] = send(zs.at[2, here], z2r.at[1, here], at_zh(3))
        else:
            z_c["up2", part].wait_recv()
            z_c["dn2", part].wait_recv()
            own = pl.ds(at16(base + (k * 4 + x) * rows), rows)
            gs[own, :] = (p + (z2r[0, here].astype(F32) + z2r[1, here].astype(F32))).astype(BF16)
            g_x[part] = [send(gs.at[own], gs.at[own], at_x(d)) for d in (1, 3, 2)]

    for n in range(8):
        if n + 2 < 8:
            rest_relay(n + 2)
        if n + 5 < 8:
            rest_to_y(n + 5)
        stage1(n)
        if n >= 1:
            stage2(n - 1)
        if n >= 3:
            stage3(n - 3)
        if n == 3:
            w_to_core(0)
        if n == 5:
            w_zc["up"].wait_recv()
            w_z("up3", 3, 2, 0, 48, 1)
            w_zc["dn"].wait_recv()
            w_z("dn3", 1, 2, 48, 32, 3)
    stage2(7)
    w_zc["dn2"].wait_recv()
    w_to_x(1)
    stage3(5)
    stage3(6)

    def dh_step(o, first):
        @pl.loop(0, 2)
        def _(i):
            c = cot[o, pl.ds(i * 2, 2)].reshape(256, CB)
            t = jnp.dot(c, wt[o].reshape(CB, BR), preferred_element_type=F32)
            rows = pl.ds(pl.multiple_of(i * 256, 256), 256)
            if first:
                acc[rows, :] = t
            else:
                acc[rows, :] += t

    w_core[0].wait_recv()
    dh_step(0, True)

    stage3(7)
    w_zc["up2"].wait_recv()
    w_to_x(3)
    w_zc["up3"].wait_recv()
    w_zc["dn3"].wait_recv()
    g_core = []
    for part in (0, 1):
        for c in g_x[part]:
            c.wait_recv()
        base, rows = PARTS[part][3:5]
        half = pl.ds(at16(base + k * (4 * rows)), 4 * rows)
        g_core.append(send(gs.at[half], gs.at[half], at_core()))
    w_to_core(1)
    w_to_x(2)
    for part in (0, 1):
        g_core[part].wait_recv()
        c0, cols, tiles, base = PARTS[part][:4]
        for j in range(tiles):
            g2[:, c0 + j * 128:c0 + (j + 1) * 128] = gs[pl.ds(base + j * 800, 800), :]

    def pick(n, per_zh, per_x, per_k, first, used):
        r = lax.broadcasted_iota(jnp.int32, (48, n), 1)
        i = lax.broadcasted_iota(jnp.int32, (48, n), 0) - first
        base = x * per_x + k * per_k
        parts = []
        for e in range(4):
            hit = jnp.logical_and(r == i + (base + ((zh + e) % 4) * per_zh), jnp.logical_and(i >= 0, i < used))
            parts.append(hit.astype(F32))
        return jnp.concatenate(parts, axis=0).astype(BF16)

    gm = g2[...]
    rows_l = jnp.dot(pick(BR, 200, 50, 25, 0, 25), gm, preferred_element_type=F32).astype(BF16)
    lt = lax.dot_general(rows_l, gm, (((1,), (1,)), ((), ())), preferred_element_type=F32) / CB
    cols_r = lax.dot_general(
        pick(CB, 160, 40, 20, 25, 20), gm, (((1,), (1,)), ((), ())), preferred_element_type=F32).astype(BF16)
    rt = jnp.dot(cols_r, gm, preferred_element_type=F32) / BR
    for e in (2, 1, 3):
        a = lt[48 * e:48 * e + 48]
        b = rt[48 * e:48 * e + 48]
        sp[e - 1, :, pl.ds(0, 640)] = (a[:, :640] + b).astype(BF16)
        tail = a[:, 768:800]
        none = jnp.zeros((25, 32), F32)
        first = jnp.concatenate([none, tail[:20], none[:3]], axis=0)
        second = jnp.concatenate([none, tail[20:25], none[:18]], axis=0)
        both = jnp.concatenate([first, second, jnp.zeros((48, 64), F32)], axis=1)
        sp[e - 1, :, pl.ds(640, 128)] = (a[:, 640:768] + both).astype(BF16)
    st = {}
    for e in (2, 1, 3):
        st[e] = send(sp.at[e - 1], rp.at[e - 1], at_zh(e))
    lt4[zh, pl.ds(0, 25), :] = lt[:25]
    rt4[zh, pl.ds(0, 20), :] = rt[25:45]
    sel = (lax.broadcasted_iota(jnp.int32, (80, CB), 1)
           == lax.broadcasted_iota(jnp.int32, (80, CB), 0) + (2 * x + k) * 80)
    gd_ref[...] = lax.dot_general(
        sel.astype(F32).astype(BF16), gm, (((1,), (1,)), ((), ())), preferred_element_type=F32).astype(BF16)

    w_core[1].wait_recv()
    dh_step(1, False)
    w_to_core(3)
    w_core[3].wait_recv()
    dh_step(3, False)
    w_to_core(2)
    w_core[2].wait_recv()
    stores = []
    for i in range(2):
        c = cot[2, pl.ds(i * 2, 2)].reshape(256, CB)
        rows = pl.ds(i * 256, 256)
        dh = (acc[rows, :] + jnp.dot(c, wt[2].reshape(CB, BR), preferred_element_type=F32)).T
        gu[:, rows] = (dh * act[:, rows]).astype(BF16)
        gg[:, rows] = (dh * fac[:, rows]).astype(BF16)
        for r in (2 * i, 2 * i + 1):
            col = pl.multiple_of(((zl + r) % 4) * 128, 128)
            a = pltpu.make_async_copy(gg.at[:, pl.ds(r * 128, 128)], gg_h.at[:, pl.ds(col, 128)], lsem.at[13 + r])
            b = pltpu.make_async_copy(gu.at[:, pl.ds(r * 128, 128)], gu_h.at[:, pl.ds(col, 128)], lsem.at[17 + r])
            a.start()
            b.start()
            stores += [a, b]

    for e in (1, 3, 2):
        st[e].wait_recv()
        c = (zh + 4 - e) % 4
        v = rp[e - 1].astype(F32)
        lt4[c, pl.ds(0, 25), pl.ds(0, 768)] = v[:25]
        lt4[c, pl.ds(0, 20), pl.ds(768, 32)] = v[25:45, 640:672]
        lt4[c, pl.ds(20, 5), pl.ds(768, 32)] = v[25:30, 672:704]
        rt4[c, pl.ds(0, 20), :] = v[25:45, :640]
    for c in range(4):
        left_ref[:, c, :] = lt4[c, pl.ds(0, 25), :]
        right_ref[:, c, :] = rt4[c, pl.ds(0, 20), :]

    for c in stores:
        c.wait()
    for c in sent:
        c.wait_send()
    for o in ORDER:
        for j in (1, 2, 3):
            for d in (1, -1):
                @pl.when(line_sends(o, j, d))
                def _(o=o, j=j, d=d):
                    line_copy(o, j, d).wait_send()
    assert count[0] <= NSEM


def place(*refs):
    n = len(refs) // 3
    held, sem = refs[2 * n:3 * n], refs[3 * n]
    into = [pltpu.make_async_copy(refs[i], held[i], sem.at[i]) for i in range(n)]
    out = [pltpu.make_async_copy(held[i], refs[n + i], sem.at[n + i]) for i in range(n)]
    for c in into:
        c.start()
    for c, d in zip(into, out):
        c.wait()
        d.start()
    for d in out:
        d.wait()


def body(gate_pre, up_pre, cotangent, down_weight):
    anyspec = pl.BlockSpec(memory_space=pl.ANY)
    vspec = pl.BlockSpec(memory_space=pltpu.VMEM)
    v = pltpu.VMEM
    out = pl.pallas_call(
        kernel,
        out_shape=(
            jax.ShapeDtypeStruct((BR, TOK), BF16),
            jax.ShapeDtypeStruct((BR, TOK), BF16),
            jax.ShapeDtypeStruct((80, BR), BF16),
            jax.ShapeDtypeStruct((25, 4, BR), F32),
            jax.ShapeDtypeStruct((20, 4, CB), F32),
        ),
        in_specs=[anyspec] * 4,
        out_specs=(anyspec, anyspec, vspec, vspec, vspec),
        scratch_shapes=[
            v((BR, TOK), BF16),
            v((BR, TOK), BF16),
            v((4, 4, 4, 32, CB), BF16),
            v((BR, TOK), BF16),
            v((BR, TOK), F32),
            v((BR, TOK), F32),
            v((4, 4, 2, 80, BR), BF16),
            v((4, 4096, 128), BF16),
            v((4, 2048, 128), BF16),
            v((4, 2048, 128), BF16),
            v((4, 3, 512, 128), BF16),
            v((3, 512, 128), BF16),
            v((2, 512, 128), BF16),
            v((2, 512, 128), BF16),
            v((4096, 128), BF16),
            v((BR, CB), BF16),
            v((3, 48, 768), BF16),
            v((3, 48, 768), BF16),
            v((4, 32, BR), F32),
            v((4, 32, CB), F32),
            v((TOK, BR), F32),
            v((BR, TOK), BF16),
            v((BR, TOK), BF16),
            pltpu.SemaphoreType.DMA((NSEM,)),
            pltpu.SemaphoreType.DMA((NSEM,)),
            pltpu.SemaphoreType.DMA((21,)),
        ],
        compiler_params=pltpu.CompilerParams(
            collective_id=0, has_side_effects=True, vmem_limit_bytes=56 * 2**20),
        cost_estimate=pl.CostEstimate(flops=4_600_000_000, bytes_accessed=6_000_000, transcendentals=410_000),
    )(gate_pre.T, up_pre.T, cotangent, down_weight.T)
    out = pl.pallas_call(
        place,
        out_shape=tuple(jax.ShapeDtypeStruct(o.shape, o.dtype) for o in out),
        in_specs=[anyspec] * 5,
        out_specs=(anyspec,) * 5,
        scratch_shapes=[v(o.shape, o.dtype) for o in out] + [pltpu.SemaphoreType.DMA((10,))],
        compiler_params=pltpu.CompilerParams(vmem_limit_bytes=56 * 2**20),
    )(*out)
    return (out[0].T, out[1].T, out[2].T,
            out[3].transpose(1, 0, 2)[None], out[4].transpose(1, 0, 2)[None])


def solution(mesh):
    return jax.shard_map(
        body,
        mesh=mesh,
        in_specs=(
            P("dp", "tensor"),
            P("dp", "tensor"),
            P(("dp", "tensor"), None),
            P("tensor", "dp"),
        ),
        out_specs=(
            P("dp", "tensor"),
            P("dp", "tensor"),
            P("tensor", "dp"),
            P("tensor", None, "dp", None),
            P("tensor", None, "dp", None),
        ),
        check_vma=False,
    )
```

time: 115 us -> 102 us (0.89)
  local copies, waits for them, and re-layouts: 11.2 us -> 0 us
  Pallas kernels: 103 us -> 101 us
    unnamed x18 -> x0, local copies, waits for them, and re-layouts: 11.2 us -> none
    pallas_call x1 -> x2, Pallas kernels: 103 us -> 101 us  [the longest x1 98.1 us: body(): pl.pallas_call(kernel, out_shape=(jax.ShapeDtypeStruct((BR, TOK), BF16),...]
where the time goes in v2:
time: 102 us; the launch traced here: 101 us
  Pallas kernels  101 us (99%)
    pallas_call x1, Pallas kernels, body(): pl.pallas_call(kernel, out_shape=(jax.ShapeDtypeStruct((BR, TOK), BF16),...  98.1 us
    pallas_call x1, Pallas kernels, body(): pl.pallas_call(place, out_shape=tuple((jax.ShapeDtypeStruct(o.shape, o.dt...  2.62 us

profile of v2, /device:TPU:1, one launch (start us, length us, event | category | flops | bytes accessed | tf_op | source)
XLA Modules:
  0.0 101.4 jit_solution(3285493115911694794)
XLA Ops:
  0.6 98.1 %shard_map.83 = (bf16[800,512]{1,0:T(8,128)(2,1)}, bf16[800,512]{1,0:T(8,128)(2,1)}, bf16[80,800]{1,0:T(8,128)(2,1)}, f32[25,4,800]{2,1,0:T(4,128)}, f32[20,4,640]{2,1,0:T(4,128)}) custom-call(bf16[800,512]{1,0:T(8,128)(2,1)} %bitcast.12, bf16[800,512]{1,0:T(8,128)(2,1)} %bitcast.13, bf16[32,2560]{1,0:T(8,128)(2,1)} %cot_h.1, bf16[80,800]{1,0:T(8,128)(2,1)} %bitcast.18), custom_call_target="tpu_custom_call" | custom-call | flops 4600000000 | bytes 6000000 | tf_op jit(solution)/shard_map/pallas_call | solution.py:476
  98.8 2.6 %shard_map.84 = (bf16[800,512]{1,0:T(8,128)(2,1)}, bf16[800,512]{1,0:T(8,128)(2,1)}, bf16[80,800]{1,0:T(8,128)(2,1)}, f32[25,4,800]{2,1,0:T(4,128)}, f32[20,4,640]{2,1,0:T(4,128)}) custom-call(bf16[800,512]{1,0:T(8,128)(2,1)} %get-tuple-element.15.refs_0_, bf16[800,512]{1,0:T(8,128)(2,1)} %get-tuple-element.16.refs_1_, ...), custom_call_target="tpu_custom_call" | custom-call | tf_op jit(solution)/shard_map/pallas_call | solution.py:519

commit v3 on v2

--- a/solution.py
+++ b/solution.py
@@ -332,9 +332,12 @@
             w_z("up3", 3, 2, 0, 48, 1)
             w_zc["dn"].wait_recv()
             w_z("dn3", 1, 2, 48, 32, 3)
+        if n == 6:
+            w_zc["dn2"].wait_recv()
+            w_to_x(1)
     stage2(7)
-    w_zc["dn2"].wait_recv()
-    w_to_x(1)
+    w_zc["up2"].wait_recv()
+    w_to_x(3)
     stage3(5)
     stage3(6)
 
@@ -353,10 +356,10 @@
     dh_step(0, True)
 
     stage3(7)
-    w_zc["up2"].wait_recv()
-    w_to_x(3)
     w_zc["up3"].wait_recv()
     w_zc["dn3"].wait_recv()
+    w_to_x(2)
+    w_to_core(1)
     g_core = []
     for part in (0, 1):
         for c in g_x[part]:
@@ -364,8 +367,7 @@
         base, rows = PARTS[part][3:5]
         half = pl.ds(at16(base + k * (4 * rows)), 4 * rows)
         g_core.append(send(gs.at[half], gs.at[half], at_core()))
-    w_to_core(1)
-    w_to_x(2)
+    w_to_core(3)
     for part in (0, 1):
         g_core[part].wait_recv()
         c0, cols, tiles, base = PARTS[part][:4]
@@ -410,7 +412,6 @@
 
     w_core[1].wait_recv()
     dh_step(1, False)
-    w_to_core(3)
     w_core[3].wait_recv()
     dh_step(3, False)
     w_to_core(2)

time: 102 us -> 107 us (1.049)
  Pallas kernels: 101 us -> 106 us
    pallas_call x1, Pallas kernels: 98.1 us -> 103 us  [body(): pl.pallas_call(kernel, out_shape=(jax.ShapeDtypeStruct((BR, TOK), BF16),...]
where the time goes in v3:
time: 107 us
  Pallas kernels  106 us (99%)
    pallas_call x1, Pallas kernels, body(): pl.pallas_call(kernel, out_shape=(jax.ShapeDtypeStruct((BR, TOK), BF16),...  103 us
    pallas_call x1, Pallas kernels, body(): pl.pallas_call(place, out_shape=tuple((jax.ShapeDtypeStruct(o.shape, o.dt...  2.62 us

profile of v3, /device:TPU:1, one launch (start us, length us, event | category | flops | bytes accessed | tf_op | source)
XLA Modules:
  0.0 106.6 jit_solution(3623027113723464416)
XLA Ops:
  0.6 103.3 %shard_map.83 = (bf16[800,512]{1,0:T(8,128)(2,1)}, bf16[800,512]{1,0:T(8,128)(2,1)}, bf16[80,800]{1,0:T(8,128)(2,1)}, f32[25,4,800]{2,1,0:T(4,128)}, f32[20,4,640]{2,1,0:T(4,128)}) custom-call(bf16[800,512]{1,0:T(8,128)(2,1)} %bitcast.12, bf16[800,512]{1,0:T(8,128)(2,1)} %bitcast.13, bf16[32,2560]{1,0:T(8,128)(2,1)} %cot_h.1, bf16[80,800]{1,0:T(8,128)(2,1)} %bitcast.18), custom_call_target="tpu_custom_call" | custom-call | flops 4600000000 | bytes 6000000 | tf_op jit(solution)/shard_map/pallas_call | solution.py:477
  103.9 2.6 %shard_map.84 = (bf16[800,512]{1,0:T(8,128)(2,1)}, bf16[800,512]{1,0:T(8,128)(2,1)}, bf16[80,800]{1,0:T(8,128)(2,1)}, f32[25,4,800]{2,1,0:T(4,128)}, f32[20,4,640]{2,1,0:T(4,128)}) custom-call(bf16[800,512]{1,0:T(8,128)(2,1)} %get-tuple-element.15.refs_0_, bf16[800,512]{1,0:T(8,128)(2,1)} %get-tuple-element.16.refs_1_, ...), custom_call_target="tpu_custom_call" | custom-call | tf_op jit(solution)/shard_map/pallas_call | solution.py:520
